TPU v7x, 256 devices: a whole 4x4x8 slice. The times are simulated.
256 devices in a mesh: dp: 32 (over x_lo, z, core), section: 8 (over y, x_hi).
Axes of the slice: x: 4 (x_hi: 2, x_lo: 2; x = x_hi * 2 + x_lo), y: 4, z: 8, core: 2. Of those that a mesh axis runs over, the one named last changes fastest.
Arguments:
- noise: bfloat16 [128, 64, 1536], P('dp'), may hold values from -6 to 6
- sched_index: int32 [128, 3], P('dp'), may hold values from 0 to 1000, as said below
- text_ids: int32 [128, 77], replicated, may hold values from 0 to 49407
- text_table: bfloat16 [49408, 1536], P('dp'), may hold values from -24 to 24
- time_weight: bfloat16 [256, 1536], replicated, may hold values from -0.375 to 0.375
- block_weight: bfloat16 [8, 1536, 1536], P('section', 'dp'), may hold values from -0.15625 to 0.15625
- block_mod: float32 [8, 3, 1536], P('section'), may hold values from -3 to 3
- student_weight: bfloat16 [1536, 1536], P('dp', 'section'), may hold values from -0.15625 to 0.15625
- student_mod: float32 [3, 1536], replicated, may hold values from -3 to 3
- feature_weight: bfloat16 [1536, 512], P('section'), may hold values from -0.15625 to 0.15625
- lin_weight: float32 [512], replicated, may hold values from 0.01 to 0.1
- token_weight: float32 [8192], P('dp'), may hold values from 0.5 to 2
Outputs:
- teacher_latents: bfloat16 [128, 64, 1536], P('dp')
- student_grad: float32 [1536, 1536], P(None, 'section')
- token_distance: float32 [8192], P(('dp', 'section'))
Inputs may be any that keep to these rules, and one draw needn't show every extreme that they name: `sched_index`: each row falls strictly from left to right, by 62 to 250 a step, and starts at 500 or higher.
All inputs are finite; a program needn't handle non-finite values.
Results may differ from a plain program's by a relative error of at most 0.024.
Values may be sent and summed in bfloat16 or wider, within the bound.
A program may use at most 64 MiB of HBM per device.

v0:
```python
import math
import jax
import jax.numpy as jnp
from jax import lax
from jax.sharding import Mesh
from jax.sharding import PartitionSpec as P

LEVELS = 1000
DP = ("dp_0", "dp_1", "dp_2")
DP_SECTION = ("dp_0", "dp_1", "dp_2", "section")


def in_blocks(x, dim, count):
    shape = x.shape
    blocks = x.reshape(*shape[:dim], count, shape[dim] // count, *shape[dim + 1 :])
    return jnp.moveaxis(blocks, dim, 0)


def summed_on_arrival(x, axis, dim):
    blocks = in_blocks(x, dim, lax.axis_size(axis))
    arrived = lax.all_to_all(blocks, axis, split_axis=0, concat_axis=0, tiled=True)
    return arrived.sum(axis=0)


def from_behind(block, axis, distance):
    devices = range(lax.axis_size(axis))
    route = [((i - distance) % len(devices), i) for i in devices]
    return lax.ppermute(block, axis, route)


def picked(x, axis, root):
    return lax.dynamic_index_in_dim(lax.all_gather(x, axis), root, 0, keepdims=False)


def in_order(blocks, dim):
    blocks = jnp.moveaxis(blocks, 0, dim)
    shape = blocks.shape
    return blocks.reshape(*shape[:dim], shape[dim] * shape[dim + 1], *shape[dim + 2 :])


def from_everyone(x, axis):
    copies = jnp.broadcast_to(x, (lax.axis_size(axis), *x.shape))
    return lax.all_to_all(copies, axis, split_axis=0, concat_axis=0, tiled=True)


def collect(x, axis, dim):
    return in_order(from_everyone(x, axis), dim)


def sum_at_owner(x, axis, dim):
    blocks = in_blocks(x, dim, lax.axis_size(axis))
    arrived = lax.all_to_all(blocks, axis, split_axis=0, concat_axis=0, tiled=True)
    return arrived.astype(jnp.float32).sum(axis=0)


def side_by_side(arrays, axis, dim, along):
    widths = [a.shape[along] for a in arrays]
    both = jnp.concatenate(arrays, axis=along)
    result = sum_at_owner(both, axis, dim)
    return tuple(jnp.split(result, [sum(widths[:k]) for k in range(1, len(widths))], axis=along))


def filled_up(lines, count):
    spare = -len(lines) % count
    return jnp.pad(lines, [(0, spare)] + [(0, 0)] * (lines.ndim - 1))


def gather_axes(x, axes, dim):
    far, near = axes
    initial = from_everyone(x, far)
    blocks = jnp.swapaxes(from_everyone(initial, near), 0, 1)
    return in_order(blocks.reshape(-1, *x.shape), dim)


def summed_rows(x, axes, dim):
    far, near = axes
    own = sum_at_owner(in_blocks(x, dim, lax.axis_size(far)), near, dim + 1)
    return jnp.sum(
        lax.all_to_all(own.astype(jnp.bfloat16), far, 0, 0, tiled=True).astype(jnp.float32), axis=0
    )


def sum_by_parts(x, axes):
    lines = x.reshape(-1, x.shape[-1])
    padded = filled_up(lines, lax.axis_size(axes[0]) * lax.axis_size(axes[1]))
    whole = gather_axes(summed_rows(padded, axes, 0).astype(jnp.bfloat16), axes, 0)
    return lax.slice_in_dim(whole, 0, len(lines)).reshape(x.shape).astype(jnp.float32)


def modulated(hidden_f, cond_vec, gains):
    mean_sq = jnp.mean(hidden_f * hidden_f, axis=-1, keepdims=True)
    normed = hidden_f * lax.rsqrt(mean_sq + 1e-06)
    return normed * (1.0 + cond_vec * gains[0]) + cond_vec * gains[1]


def teacher_block(hidden, weight, gains, cond_vec):
    hidden_f = hidden.astype(jnp.float32)
    inputs = modulated(hidden_f, cond_vec, gains).astype(jnp.bfloat16)
    mixed = jnp.dot(inputs, weight, preferred_element_type=jnp.float32)
    return (hidden_f + (1.0 + cond_vec * gains[2]) * jax.nn.gelu(mixed)).astype(jnp.bfloat16)


def distance(feat_student, feat_teacher, lin_weight):
    relu_s = jax.nn.relu(feat_student)
    relu_t = jax.nn.relu(feat_teacher)
    unit_s = relu_s * lax.rsqrt(jnp.mean(relu_s * relu_s, axis=-1, keepdims=True) + 1e-06)
    unit_t = relu_t * lax.rsqrt(jnp.mean(relu_t * relu_t, axis=-1, keepdims=True) + 1e-06)
    gap = unit_s - unit_t
    return jnp.sum(lin_weight * gap * gap, axis=-1)


def store(buffer, value, valid, slot_id):
    old_value = lax.dynamic_index_in_dim(buffer, slot_id, 0, keepdims=False)
    return lax.dynamic_update_index_in_dim(buffer, jnp.where(valid, value, old_value), slot_id, 0)


def local(
    noise,
    sched_index,
    text_ids,
    text_table,
    time_weight,
    block_weight,
    block_mod,
    student_weight,
    student_mod,
    feature_weight,
    lin_weight,
    token_weight,
):
    batches, tokens, model_width = noise.shape
    steps = sched_index.shape[1] - 1
    sections = lax.axis_size("section")
    own_section = lax.axis_index("section")
    vocab_rows = text_table.shape[0]
    offset = lax.axis_index(DP) * vocab_rows
    text_len = text_ids.shape[1]
    local_ids = text_ids - offset
    vocab_ids = jnp.arange(vocab_rows, dtype=jnp.int32)

    def add_group(group_id, counts):
        id_block = lax.dynamic_slice_in_dim(local_ids, group_id * 7, 7, 1)
        return counts + jnp.sum((id_block[:, :, None] == vocab_ids).astype(jnp.float32), axis=1)

    counts = lax.fori_loop(
        0,
        text_len // 7,
        add_group,
        jnp.zeros((batches * lax.axis_size(DP), vocab_rows), jnp.float32),
    )
    pooled = summed_on_arrival(
        jnp.dot(counts.astype(jnp.bfloat16), text_table, preferred_element_type=jnp.float32)
        / text_len,
        DP,
        0,
    )
    weights = lax.all_gather(block_weight, DP, axis=1, tiled=True)[0]
    section_mod = block_mod[0]
    indices_f = sched_index.astype(jnp.float32)
    half_freq = time_weight.shape[0] // 2
    frequency = jnp.exp(-math.log(10000.0) * jnp.arange(half_freq, dtype=jnp.float32) / half_freq)
    angles = indices_f[:, :, None] * frequency
    embedding = jnp.concatenate([jnp.cos(angles), jnp.sin(angles)], axis=-1).astype(jnp.bfloat16)
    time_embed = jnp.dot(
        embedding.reshape(-1, 2 * half_freq), time_weight, preferred_element_type=jnp.float32
    )
    conditions = jax.nn.silu(
        time_embed.reshape(batches, steps + 1, model_width) + pooled[:, None, :]
    )
    deltas = (indices_f[:, 1:] - indices_f[:, :-1]) / LEVELS
    surplus = max(0, batches - sections)
    period = sections + surplus
    tick_count = steps * sections + batches - 1 + (steps - 1) * surplus
    sender = (own_section + sections - 1) % sections

    def locate(section_at, tick_now):
        active = jnp.zeros((), jnp.bool_)
        slot_id = jnp.zeros((), jnp.int32)
        pass_id = jnp.zeros((), jnp.int32)
        for pass_now in range(steps):
            candidate = tick_now - section_at - pass_now * period
            fits = (candidate >= 0) & (candidate < batches)
            slot_id = jnp.where(fits, candidate, slot_id)
            pass_id = jnp.where(fits, pass_now, pass_id)
            active = active | fits
        return (active, slot_id, pass_id)

    def run_block(active, hidden, cond_vec):
        return lax.cond(
            active,
            lambda hidden_in: teacher_block(hidden_in, weights, section_mod, cond_vec),
            lambda hidden_in: hidden_in,
            hidden,
        )

    def tick_entry(tick_now, buffers):
        arrived, iterates = buffers
        active, slot_id, pass_id = locate(own_section, tick_now)
        hidden = lax.dynamic_index_in_dim(arrived, slot_id, 0, keepdims=False)
        start_x = lax.dynamic_index_in_dim(iterates, slot_id, 0, keepdims=False)
        is_first = own_section == 0
        step_size = deltas[slot_id, jnp.maximum(pass_id - 1, 0)]
        advanced = (start_x.astype(jnp.float32) + step_size * hidden.astype(jnp.float32)).astype(
            jnp.bfloat16
        )
        hidden = jnp.where(is_first & (pass_id >= 1), advanced, hidden)
        iterates = store(iterates, hidden, is_first & active, slot_id)
        result = run_block(active, hidden, conditions[slot_id, pass_id])
        got_hidden = from_behind(result, "section", 1)
        valid, source, unused = locate(sender, tick_now)
        arrived = store(arrived, got_hidden, valid, source)
        return (arrived, iterates)

    arrived, iterates = lax.fori_loop(0, tick_count, tick_entry, (noise, noise))
    latest = (
        iterates.astype(jnp.float32)
        + deltas[:, steps - 1][:, None, None] * arrived.astype(jnp.float32)
    ).astype(jnp.bfloat16)
    root_section = 0
    teacher = picked(latest, "section", root_section)
    col_count = student_weight.shape[1]
    first_col = own_section * col_count
    row_count = batches * tokens
    noise_f = noise.astype(jnp.float32)
    cond_zero = conditions[:, 0][:, None, :]
    time_zero = (indices_f[:, 0] / LEVELS)[:, None, None]
    inputs = (
        modulated(noise_f, cond_zero, student_mod)
        .astype(jnp.bfloat16)
        .reshape(row_count, model_width)
    )
    mixed = jnp.dot(inputs, collect(student_weight, DP, 0), preferred_element_type=jnp.float32)
    z_cols = lax.dynamic_slice_in_dim(noise_f, first_col, col_count, 2).reshape(
        row_count, col_count
    )
    gate_full = 1.0 + cond_zero * student_mod[2]
    gate_rows = jnp.broadcast_to(
        lax.dynamic_slice_in_dim(gate_full, first_col, col_count, 2), (batches, tokens, col_count)
    ).reshape(row_count, col_count)
    t_rows = jnp.broadcast_to(time_zero, (batches, tokens, 1)).reshape(row_count, 1)

    def advance(mixed_in):
        return z_cols - t_rows * (z_cols + gate_rows * jax.nn.gelu(mixed_in))

    moved, pull_back = jax.vjp(advance, mixed)
    feat_student = jnp.dot(
        moved.astype(jnp.bfloat16), feature_weight, preferred_element_type=jnp.float32
    )
    target_cols = lax.dynamic_slice_in_dim(teacher, first_col, col_count, 2).reshape(
        row_count, col_count
    )
    feat_teacher = jnp.dot(target_cols, feature_weight, preferred_element_type=jnp.float32)
    share_rows = row_count // sections
    part_student, part_teacher = side_by_side(
        (feat_student.astype(jnp.bfloat16), feat_teacher.astype(jnp.bfloat16)), "section", 0, 1
    )
    weight_share = lax.dynamic_slice_in_dim(token_weight, own_section * share_rows, share_rows, 0)

    def objective(feat_in):
        token_dist = distance(feat_in, part_teacher, lin_weight)
        return (jnp.sum(weight_share * token_dist), token_dist)

    total, pull_feat, token_distance = jax.vjp(objective, part_student, has_aux=True)
    grad_share = pull_feat(jnp.ones_like(total))[0].astype(jnp.bfloat16)
    grad_feat = collect(grad_share, "section", 0)
    out_grad = lax.dot_general(
        grad_feat, feature_weight, (((1,), (1,)), ((), ())), preferred_element_type=jnp.float32
    )
    mixed_grad = pull_back(out_grad)[0].astype(jnp.bfloat16)
    partial_grad = lax.dot_general(
        inputs, mixed_grad, (((0,), (0,)), ((), ())), preferred_element_type=jnp.float32
    )
    student_grad = sum_by_parts(partial_grad.astype(jnp.bfloat16), (("dp_0", "dp_1"), "dp_2"))
    return (teacher, student_grad, token_distance)


def solution(mesh):
    torus = Mesh(
        mesh.devices.reshape(2, 8, 2, mesh.shape["section"]), ("dp_0", "dp_1", "dp_2", "section")
    )
    in_specs = (
        P(DP, None, None),
        P(DP, None),
        P(),
        P(DP, None),
        P(),
        P("section", DP, None),
        P("section", None, None),
        P(DP, "section"),
        P(),
        P("section", None),
        P(),
        P(DP),
    )
    out_specs = (P(DP, None, None), P(None, "section"), P(DP_SECTION))
    return jax.shard_map(local, mesh=torus, in_specs=in_specs, out_specs=out_specs, check_vma=False)
```

profile of v0, /device:TPU:1, one launch (start us, length us, event | category | flops | bytes accessed | tf_op | source)
XLA Modules:
  0.0 550.5 jit_solution(15804008191292427286)
XLA Ops:
  8.7 10.4 %while.33 = (s32[]{:T(128)}, f32[128,1544]{0,1:T(8,128)S(1)}, s32[128,77]{0,1:T(8,128)S(1)}, s32[]{:T(128)}, s32[]{:T(128)}, /*index=5*/s32[]{:T(128)}, s32[]{:T(128)}) while((s32[]{:T(128)}, f32[128,1544]{0,1:T(8,128)S(1)}, s32[128,77]{0,1:T(8,128)S(1)}, s32[]{:T(128)}, s32[]{:T(128)}, /*index=5*/s32[]{:T(128)}, s32[]{:T(128)}) %tuple.112), condition=%wide.region_2.0_spmd.clone, body=%wide.region_0.0_spmd.clone.sunk | while | flops 4347911 | bytes 3173001 | solution.py:145
  23.5 11.1 %all-to-all-start = ((f32[32,4,1536]{2,1,0:T(4,128)}), f32[32,4,1536]{2,1,0:T(4,128)}, u32[]{:S(2)}, u32[]{:S(2)}) async-start(f32[32,4,1536]{2,1,0:T(4,128)} %reshape.121), calls=%async_computation | async-start | bytes 1572864 | tf_op jit(solution)/shard_map/all_to_all | solution.py:21
  36.3 26.8 %all-to-all-done = f32[32,4,1536]{2,1,0:T(4,128)} async-done(((f32[32,4,1536]{2,1,0:T(4,128)}), f32[32,4,1536]{2,1,0:T(4,128)}, u32[]{:S(2)}, u32[]{:S(2)}) %all-to-all-start) | async-done | bytes 786464 | tf_op jit(solution)/shard_map/all_to_all | solution.py:21
  65.9 24.6 %all-gather.4.cloned.1.call-done = bf16[1,1536,1536]{2,1,0:T(8,128)(2,1)} async-done(((bf16[1,48,1536]{2,1,0:T(8,128)(2,1)}), bf16[1,1536,1536]{2,1,0:T(8,128)(2,1)}) %all-gather.4.cloned.1.call-update) | async-done | bytes 4718608 | tf_op jit(solution)/shard_map/all_gather | solution.py:157
  90.5 258.7 %while.32 = (s32[]{:T(128)}, bf16[4,64,1536]{2,1,0:T(8,128)(2,1)S(1)}, bf16[4,64,1536]{2,1,0:T(8,128)(2,1)S(1)}, s32[]{:T(128)}, s32[]{:T(128)}, /*index=5*/pred...) while((s32[]{:T(128)}, ...), condition=%wide.region_8.9_spmd, body=%wide.region_4.8_spmd.sunk | while | flops 305340000 | bytes 8762968 | solution.py:214
  91.9 5.3 conditional.2
  97.3 9.8 %collective-permute-done = bf16[64,1536]{1,0:T(8,128)(2,1)S(1)} collective-permute-done((bf16[64,1536]{1,0:T(8,128)(2,1)S(1)}, bf16[64,1536]{1,0:T(8,128)(2,1)S(1)}, u32[]{:S(2)}, u32[]{:S(2)}) %collective-permute-start) | collective-permute-done | bytes 196640 | tf_op jit(solution)/shard_map/while/body/eval_jaxpr/ppermute | solution.py:28
  109.4 5.3 conditional.2
  114.8 8.9 %collective-permute-done = bf16[64,1536]{1,0:T(8,128)(2,1)S(1)} collective-permute-done((bf16[64,1536]{1,0:T(8,128)(2,1)S(1)}, bf16[64,1536]{1,0:T(8,128)(2,1)S(1)}, u32[]{:S(2)}, u32[]{:S(2)}) %collective-permute-start) | collective-permute-done | bytes 196640 | tf_op jit(solution)/shard_map/while/body/eval_jaxpr/ppermute | solution.py:28
  126.0 5.3 conditional.2
  131.4 8.1 %collective-permute-done = bf16[64,1536]{1,0:T(8,128)(2,1)S(1)} collective-permute-done((bf16[64,1536]{1,0:T(8,128)(2,1)S(1)}, bf16[64,1536]{1,0:T(8,128)(2,1)S(1)}, u32[]{:S(2)}, u32[]{:S(2)}) %collective-permute-start) | collective-permute-done | bytes 196640 | tf_op jit(solution)/shard_map/while/body/eval_jaxpr/ppermute | solution.py:28
  141.7 5.3 conditional.2
  143.6 3.4 fusion.6
  147.2 8.1 %collective-permute-done = bf16[64,1536]{1,0:T(8,128)(2,1)S(1)} collective-permute-done((bf16[64,1536]{1,0:T(8,128)(2,1)S(1)}, bf16[64,1536]{1,0:T(8,128)(2,1)S(1)}, u32[]{:S(2)}, u32[]{:S(2)}) %collective-permute-start) | collective-permute-done | bytes 196640 | tf_op jit(solution)/shard_map/while/body/eval_jaxpr/ppermute | solution.py:28
  160.8 5.0 collective-permute-done
  169.2 7.1 %collective-permute-done = bf16[64,1536]{1,0:T(8,128)(2,1)S(1)} collective-permute-done((bf16[64,1536]{1,0:T(8,128)(2,1)S(1)}, bf16[64,1536]{1,0:T(8,128)(2,1)S(1)}, u32[]{:S(2)}, u32[]{:S(2)}) %collective-permute-start) | collective-permute-done | bytes 196640 | tf_op jit(solution)/shard_map/while/body/eval_jaxpr/ppermute | solution.py:28
  180.4 6.4 %collective-permute-done = bf16[64,1536]{1,0:T(8,128)(2,1)S(1)} collective-permute-done((bf16[64,1536]{1,0:T(8,128)(2,1)S(1)}, bf16[64,1536]{1,0:T(8,128)(2,1)S(1)}, u32[]{:S(2)}, u32[]{:S(2)}) %collective-permute-start) | collective-permute-done | bytes 196640 | tf_op jit(solution)/shard_map/while/body/eval_jaxpr/ppermute | solution.py:28
  189.6 7.6 %collective-permute-done = bf16[64,1536]{1,0:T(8,128)(2,1)S(1)} collective-permute-done((bf16[64,1536]{1,0:T(8,128)(2,1)S(1)}, bf16[64,1536]{1,0:T(8,128)(2,1)S(1)}, u32[]{:S(2)}, u32[]{:S(2)}) %collective-permute-start) | collective-permute-done | bytes 196640 | tf_op jit(solution)/shard_map/while/body/eval_jaxpr/ppermute | solution.py:28
  199.5 5.3 conditional.2
  201.4 3.4 fusion.6
  205.0 8.1 %collective-permute-done = bf16[64,1536]{1,0:T(8,128)(2,1)S(1)} collective-permute-done((bf16[64,1536]{1,0:T(8,128)(2,1)S(1)}, bf16[64,1536]{1,0:T(8,128)(2,1)S(1)}, u32[]{:S(2)}, u32[]{:S(2)}) %collective-permute-start) | collective-permute-done | bytes 196640 | tf_op jit(solution)/shard_map/while/body/eval_jaxpr/ppermute | solution.py:28
  215.3 5.3 conditional.2
  217.2 3.4 fusion.6
  220.8 8.1 %collective-permute-done = bf16[64,1536]{1,0:T(8,128)(2,1)S(1)} collective-permute-done((bf16[64,1536]{1,0:T(8,128)(2,1)S(1)}, bf16[64,1536]{1,0:T(8,128)(2,1)S(1)}, u32[]{:S(2)}, u32[]{:S(2)}) %collective-permute-start) | collective-permute-done | bytes 196640 | tf_op jit(solution)/shard_map/while/body/eval_jaxpr/ppermute | solution.py:28
  231.1 5.3 conditional.2
  233.0 3.4 fusion.6
  236.5 8.1 %collective-permute-done = bf16[64,1536]{1,0:T(8,128)(2,1)S(1)} collective-permute-done((bf16[64,1536]{1,0:T(8,128)(2,1)S(1)}, bf16[64,1536]{1,0:T(8,128)(2,1)S(1)}, u32[]{:S(2)}, u32[]{:S(2)}) %collective-permute-start) | collective-permute-done | bytes 196640 | tf_op jit(solution)/shard_map/while/body/eval_jaxpr/ppermute | solution.py:28
  246.9 5.3 conditional.2
  248.8 3.4 fusion.6
  252.3 8.1 %collective-permute-done = bf16[64,1536]{1,0:T(8,128)(2,1)S(1)} collective-permute-done((bf16[64,1536]{1,0:T(8,128)(2,1)S(1)}, bf16[64,1536]{1,0:T(8,128)(2,1)S(1)}, u32[]{:S(2)}, u32[]{:S(2)}) %collective-permute-start) | collective-permute-done | bytes 196640 | tf_op jit(solution)/shard_map/while/body/eval_jaxpr/ppermute | solution.py:28
  265.9 5.0 collective-permute-done
  275.3 6.1 %collective-permute-done = bf16[64,1536]{1,0:T(8,128)(2,1)S(1)} collective-permute-done((bf16[64,1536]{1,0:T(8,128)(2,1)S(1)}, bf16[64,1536]{1,0:T(8,128)(2,1)S(1)}, u32[]{:S(2)}, u32[]{:S(2)}) %collective-permute-start) | collective-permute-done | bytes 196640 | tf_op jit(solution)/shard_map/while/body/eval_jaxpr/ppermute | solution.py:28
  283.7 3.7 collective-permute-start
  287.4 4.5 collective-permute-done
  296.7 5.7 %collective-permute-done = bf16[64,1536]{1,0:T(8,128)(2,1)S(1)} collective-permute-done((bf16[64,1536]{1,0:T(8,128)(2,1)S(1)}, bf16[64,1536]{1,0:T(8,128)(2,1)S(1)}, u32[]{:S(2)}, u32[]{:S(2)}) %collective-permute-start) | collective-permute-done | bytes 196640 | tf_op jit(solution)/shard_map/while/body/eval_jaxpr/ppermute | solution.py:28
  306.0 12.7 %collective-permute-done = bf16[64,1536]{1,0:T(8,128)(2,1)S(1)} collective-permute-done((bf16[64,1536]{1,0:T(8,128)(2,1)S(1)}, bf16[64,1536]{1,0:T(8,128)(2,1)S(1)}, u32[]{:S(2)}, u32[]{:S(2)}) %collective-permute-start) | collective-permute-done | bytes 196640 | tf_op jit(solution)/shard_map/while/body/eval_jaxpr/ppermute | solution.py:28
  321.1 13.0 %collective-permute-done = bf16[64,1536]{1,0:T(8,128)(2,1)S(1)} collective-permute-done((bf16[64,1536]{1,0:T(8,128)(2,1)S(1)}, bf16[64,1536]{1,0:T(8,128)(2,1)S(1)}, u32[]{:S(2)}, u32[]{:S(2)}) %collective-permute-start) | collective-permute-done | bytes 196640 | tf_op jit(solution)/shard_map/while/body/eval_jaxpr/ppermute | solution.py:28
  336.5 11.9 %collective-permute-done = bf16[64,1536]{1,0:T(8,128)(2,1)S(1)} collective-permute-done((bf16[64,1536]{1,0:T(8,128)(2,1)S(1)}, bf16[64,1536]{1,0:T(8,128)(2,1)S(1)}, u32[]{:S(2)}, u32[]{:S(2)}) %collective-permute-start) | collective-permute-done | bytes 196640 | tf_op jit(solution)/shard_map/while/body/eval_jaxpr/ppermute | solution.py:28
  351.4 24.4 %all-to-all-start.1 = ((bf16[32,48,192]{2,1,0:T(8,128)(2,1)}), bf16[32,48,192]{2,1,0:T(8,128)(2,1)S(1)}, u32[]{:S(2)}, u32[]{:S(2)}) async-start(bf16[32,48,192]{2,1,0:T(8,128)(2,1)} %broadcast_in_dim.73), calls=%async_computation.1 | async-start | bytes 1572864 | tf_op jit(solution)/shard_map/all_to_all | solution.py:43
  381.7 15.4 %all-to-all-done.1 = bf16[32,48,192]{2,1,0:T(8,128)(2,1)S(1)} async-done(((bf16[32,48,192]{2,1,0:T(8,128)(2,1)}), bf16[32,48,192]{2,1,0:T(8,128)(2,1)S(1)}, u32[]{:S(2)}, u32[]{:S(2)}) %all-to-all-start.1) | async-done | bytes 589856 | tf_op jit(solution)/shard_map/all_to_all | solution.py:43
  397.9 66.6 %all-gather.6.cloned.1.call-done = bf16[32,64,1536]{2,1,0:T(8,128)(2,1)} async-done(((bf16[4,64,1536]{2,1,0:T(8,128)(2,1)}), bf16[32,64,1536]{2,1,0:T(8,128)(2,1)}) %all-gather.6.cloned.1.call-update) | async-done | bytes 6291472 | tf_op jit(solution)/shard_map/all_gather | solution.py:32
  466.9 3.5 all-to-all-start.2
  470.5 10.4 %all-to-all-done.2 = bf16[8,32,1024]{2,1,0:T(8,128)(2,1)S(1)} async-done(((bf16[8,32,1024]{2,1,0:T(8,128)(2,1)}), bf16[8,32,1024]{2,1,0:T(8,128)(2,1)S(1)}, u32[]{:S(2)}, u32[]{:S(2)}) %all-to-all-start.2) | async-done | bytes 524320 | tf_op jit(solution)/shard_map/all_to_all | solution.py:52
  482.0 10.3 %all_to_all.40 = bf16[8,32,512]{2,1,0:T(8,128)(2,1)S(1)} all-to-all(bf16[8,32,512]{2,1,0:T(8,128)(2,1)S(1)} %broadcast_in_dim.76), channel_id=1, replica_groups=mesh['dp_0'=2,'dp_1'=8,'dp_2'=2,'section'=8] {'section'}, dimensions={0} | all-to-all | bytes 524288 | tf_op jit(solution)/shard_map/all_to_all | solution.py:43
  493.3 7.0 %all_to_all.41 = bf16[2,16,48,192]{3,2,1,0:T(8,128)(2,1)S(1)} all-to-all(bf16[2,16,48,192]{3,2,1,0:T(8,128)(2,1)S(1)} %copy.46), channel_id=1, replica_groups=mesh['dp_0'=2,'dp_1'=8,'dp_2'=2,'section'=8] {'dp_2'}, dimensions={0} | all-to-all | bytes 1179648 | tf_op jit(solution)/shard_map/all_to_all | solution.py:52
  500.6 17.8 %all_to_all.42 = bf16[16,48,192]{2,1,0:T(8,128)(2,1)S(1)} all-to-all(bf16[16,48,192]{2,1,0:T(8,128)(2,1)S(1)} %reduce_sum.120), channel_id=1, replica_groups=mesh['dp_0'=2,'dp_1'=8,'dp_2'=2,'section'=8] {'dp_0','dp_1'}, dimensions={0} | all-to-all | bytes 589824 | tf_op jit(solution)/shard_map/all_to_all | solution.py:79
  518.5 16.9 %all_to_all.43 = bf16[16,48,192]{2,1,0:T(8,128)(2,1)S(1)} all-to-all(bf16[16,48,192]{2,1,0:T(8,128)(2,1)S(1)} %broadcast_in_dim.77), channel_id=1, replica_groups=mesh['dp_0'=2,'dp_1'=8,'dp_2'=2,'section'=8] {'dp_0','dp_1'}, dimensions={0} | all-to-all | bytes 589824 | tf_op jit(solution)/shard_map/all_to_all | solution.py:43
  535.5 6.4 %all_to_all.44 = bf16[2,16,48,192]{3,2,1,0:T(8,128)(2,1)S(1)} all-to-all(bf16[2,16,48,192]{3,2,1,0:T(8,128)(2,1)S(1)} %broadcast_in_dim.78), channel_id=1, replica_groups=mesh['dp_0'=2,'dp_1'=8,'dp_2'=2,'section'=8] {'dp_2'}, dimensions={0} | all-to-all | bytes 1179648 | tf_op jit(solution)/shard_map/all_to_all | solution.py:43
  (275 shorter events, 119.9 us)
Async XLA Ops:
  7.2 57.2 %copy-start = (bf16[256,1536]{1,0:T(8,128)(2,1)S(1)}, bf16[256,1536]{1,0:T(8,128)(2,1)}, u32[]{:S(2)}) copy-start(bf16[256,1536]{1,0:T(8,128)(2,1)} %param.22) | copy-start | bytes 2359300
  7.2 83.3 %all-gather.4.cloned.1.call-start = ((), (), s32[]{:S(2)}) async-start(), calls=%async_computation.8 | async-start | bytes 4866048 | tf_op jit(solution)/shard_map/all_gather | solution.py:157
  22.4 12.3 %copy-start.1 = (bf16[4,64,1536]{2,1,0:T(8,128)(2,1)S(1)}, bf16[4,64,1536]{2,1,0:T(8,128)(2,1)}, u32[]{:S(2)}) copy-start(bf16[4,64,1536]{2,1,0:T(8,128)(2,1)} %param.18) | copy-start | bytes 2359300
  23.5 39.6 %all-to-all-start = ((f32[32,4,1536]{2,1,0:T(4,128)}), f32[32,4,1536]{2,1,0:T(4,128)}, u32[]{:S(2)}, u32[]{:S(2)}) async-start(f32[32,4,1536]{2,1,0:T(4,128)} %reshape.121), calls=%async_computation | async-start | bytes 1572864 | tf_op jit(solution)/shard_map/all_to_all | solution.py:21
  34.6 429.8 %all-gather.6.cloned.1.call-start = ((), (), s32[]{:S(2)}) async-start(), calls=%async_computation.9 | async-start | bytes 7077888 | tf_op jit(solution)/shard_map/all_gather | solution.py:32
  34.7 0.7 copy-start.11
  34.7 0.8 copy-start.8
  34.8 55.7 %copy-start.2 = (bf16[4,64,1536]{2,1,0:T(8,128)(2,1)S(1)}, bf16[4,64,1536]{2,1,0:T(8,128)(2,1)}, u32[]{:S(2)}) copy-start(bf16[4,64,1536]{2,1,0:T(8,128)(2,1)} %param.18) | copy-start | bytes 2359300
  64.6 0.6 copy-start.6
  97.2 9.9 %collective-permute-start = (bf16[64,1536]{1,0:T(8,128)(2,1)S(1)}, bf16[64,1536]{1,0:T(8,128)(2,1)S(1)}, u32[]{:S(2)}, u32[]{:S(2)}) collective-permute-start(bf16[64,1536]{1,0:T(8,128)(2,1)S(1)} %get-tuple-element.648), channel_id=1, source_target_pairs={{7,0},{0,1},{1,2},{2,3},{3,4},{4,5},{5,6},{6,7},{15,8},{8,9},{9,10... | collective-permute-start | bytes 589832 | tf_op jit(solution)/shard_map/while/body/eval_jaxpr/ppermute | solution.py:28
  114.7 9.0 %collective-permute-start = (bf16[64,1536]{1,0:T(8,128)(2,1)S(1)}, bf16[64,1536]{1,0:T(8,128)(2,1)S(1)}, u32[]{:S(2)}, u32[]{:S(2)}) collective-permute-start(bf16[64,1536]{1,0:T(8,128)(2,1)S(1)} %get-tuple-element.648), channel_id=1, source_target_pairs={{7,0},{0,1},{1,2},{2,3},{3,4},{4,5},{5,6},{6,7},{15,8},{8,9},{9,10... | collective-permute-start | bytes 589832 | tf_op jit(solution)/shard_map/while/body/eval_jaxpr/ppermute | solution.py:28
  131.2 8.2 %collective-permute-start = (bf16[64,1536]{1,0:T(8,128)(2,1)S(1)}, bf16[64,1536]{1,0:T(8,128)(2,1)S(1)}, u32[]{:S(2)}, u32[]{:S(2)}) collective-permute-start(bf16[64,1536]{1,0:T(8,128)(2,1)S(1)} %get-tuple-element.648), channel_id=1, source_target_pairs={{7,0},{0,1},{1,2},{2,3},{3,4},{4,5},{5,6},{6,7},{15,8},{8,9},{9,10... | collective-permute-start | bytes 589832 | tf_op jit(solution)/shard_map/while/body/eval_jaxpr/ppermute | solution.py:28
  147.0 8.2 %collective-permute-start = (bf16[64,1536]{1,0:T(8,128)(2,1)S(1)}, bf16[64,1536]{1,0:T(8,128)(2,1)S(1)}, u32[]{:S(2)}, u32[]{:S(2)}) collective-permute-start(bf16[64,1536]{1,0:T(8,128)(2,1)S(1)} %get-tuple-element.648), channel_id=1, source_target_pairs={{7,0},{0,1},{1,2},{2,3},{3,4},{4,5},{5,6},{6,7},{15,8},{8,9},{9,10... | collective-permute-start | bytes 589832 | tf_op jit(solution)/shard_map/while/body/eval_jaxpr/ppermute | solution.py:28
  157.5 8.2 %collective-permute-start = (bf16[64,1536]{1,0:T(8,128)(2,1)S(1)}, bf16[64,1536]{1,0:T(8,128)(2,1)S(1)}, u32[]{:S(2)}, u32[]{:S(2)}) collective-permute-start(bf16[64,1536]{1,0:T(8,128)(2,1)S(1)} %get-tuple-element.648), channel_id=1, source_target_pairs={{7,0},{0,1},{1,2},{2,3},{3,4},{4,5},{5,6},{6,7},{15,8},{8,9},{9,10... | collective-permute-start | bytes 589832 | tf_op jit(solution)/shard_map/while/body/eval_jaxpr/ppermute | solution.py:28
  168.0 8.2 %collective-permute-start = (bf16[64,1536]{1,0:T(8,128)(2,1)S(1)}, bf16[64,1536]{1,0:T(8,128)(2,1)S(1)}, u32[]{:S(2)}, u32[]{:S(2)}) collective-permute-start(bf16[64,1536]{1,0:T(8,128)(2,1)S(1)} %get-tuple-element.648), channel_id=1, source_target_pairs={{7,0},{0,1},{1,2},{2,3},{3,4},{4,5},{5,6},{6,7},{15,8},{8,9},{9,10... | collective-permute-start | bytes 589832 | tf_op jit(solution)/shard_map/while/body/eval_jaxpr/ppermute | solution.py:28
  178.5 8.2 %collective-permute-start = (bf16[64,1536]{1,0:T(8,128)(2,1)S(1)}, bf16[64,1536]{1,0:T(8,128)(2,1)S(1)}, u32[]{:S(2)}, u32[]{:S(2)}) collective-permute-start(bf16[64,1536]{1,0:T(8,128)(2,1)S(1)} %get-tuple-element.648), channel_id=1, source_target_pairs={{7,0},{0,1},{1,2},{2,3},{3,4},{4,5},{5,6},{6,7},{15,8},{8,9},{9,10... | collective-permute-start | bytes 589832 | tf_op jit(solution)/shard_map/while/body/eval_jaxpr/ppermute | solution.py:28
  189.0 8.2 %collective-permute-start = (bf16[64,1536]{1,0:T(8,128)(2,1)S(1)}, bf16[64,1536]{1,0:T(8,128)(2,1)S(1)}, u32[]{:S(2)}, u32[]{:S(2)}) collective-permute-start(bf16[64,1536]{1,0:T(8,128)(2,1)S(1)} %get-tuple-element.648), channel_id=1, source_target_pairs={{7,0},{0,1},{1,2},{2,3},{3,4},{4,5},{5,6},{6,7},{15,8},{8,9},{9,10... | collective-permute-start | bytes 589832 | tf_op jit(solution)/shard_map/while/body/eval_jaxpr/ppermute | solution.py:28
  204.8 8.2 %collective-permute-start = (bf16[64,1536]{1,0:T(8,128)(2,1)S(1)}, bf16[64,1536]{1,0:T(8,128)(2,1)S(1)}, u32[]{:S(2)}, u32[]{:S(2)}) collective-permute-start(bf16[64,1536]{1,0:T(8,128)(2,1)S(1)} %get-tuple-element.648), channel_id=1, source_target_pairs={{7,0},{0,1},{1,2},{2,3},{3,4},{4,5},{5,6},{6,7},{15,8},{8,9},{9,10... | collective-permute-start | bytes 589832 | tf_op jit(solution)/shard_map/while/body/eval_jaxpr/ppermute | solution.py:28
  220.6 8.2 %collective-permute-start = (bf16[64,1536]{1,0:T(8,128)(2,1)S(1)}, bf16[64,1536]{1,0:T(8,128)(2,1)S(1)}, u32[]{:S(2)}, u32[]{:S(2)}) collective-permute-start(bf16[64,1536]{1,0:T(8,128)(2,1)S(1)} %get-tuple-element.648), channel_id=1, source_target_pairs={{7,0},{0,1},{1,2},{2,3},{3,4},{4,5},{5,6},{6,7},{15,8},{8,9},{9,10... | collective-permute-start | bytes 589832 | tf_op jit(solution)/shard_map/while/body/eval_jaxpr/ppermute | solution.py:28
  236.4 8.2 %collective-permute-start = (bf16[64,1536]{1,0:T(8,128)(2,1)S(1)}, bf16[64,1536]{1,0:T(8,128)(2,1)S(1)}, u32[]{:S(2)}, u32[]{:S(2)}) collective-permute-start(bf16[64,1536]{1,0:T(8,128)(2,1)S(1)} %get-tuple-element.648), channel_id=1, source_target_pairs={{7,0},{0,1},{1,2},{2,3},{3,4},{4,5},{5,6},{6,7},{15,8},{8,9},{9,10... | collective-permute-start | bytes 589832 | tf_op jit(solution)/shard_map/while/body/eval_jaxpr/ppermute | solution.py:28
  252.2 8.2 %collective-permute-start = (bf16[64,1536]{1,0:T(8,128)(2,1)S(1)}, bf16[64,1536]{1,0:T(8,128)(2,1)S(1)}, u32[]{:S(2)}, u32[]{:S(2)}) collective-permute-start(bf16[64,1536]{1,0:T(8,128)(2,1)S(1)} %get-tuple-element.648), channel_id=1, source_target_pairs={{7,0},{0,1},{1,2},{2,3},{3,4},{4,5},{5,6},{6,7},{15,8},{8,9},{9,10... | collective-permute-start | bytes 589832 | tf_op jit(solution)/shard_map/while/body/eval_jaxpr/ppermute | solution.py:28
  262.7 8.2 %collective-permute-start = (bf16[64,1536]{1,0:T(8,128)(2,1)S(1)}, bf16[64,1536]{1,0:T(8,128)(2,1)S(1)}, u32[]{:S(2)}, u32[]{:S(2)}) collective-permute-start(bf16[64,1536]{1,0:T(8,128)(2,1)S(1)} %get-tuple-element.648), channel_id=1, source_target_pairs={{7,0},{0,1},{1,2},{2,3},{3,4},{4,5},{5,6},{6,7},{15,8},{8,9},{9,10... | collective-permute-start | bytes 589832 | tf_op jit(solution)/shard_map/while/body/eval_jaxpr/ppermute | solution.py:28
  273.2 8.2 %collective-permute-start = (bf16[64,1536]{1,0:T(8,128)(2,1)S(1)}, bf16[64,1536]{1,0:T(8,128)(2,1)S(1)}, u32[]{:S(2)}, u32[]{:S(2)}) collective-permute-start(bf16[64,1536]{1,0:T(8,128)(2,1)S(1)} %get-tuple-element.648), channel_id=1, source_target_pairs={{7,0},{0,1},{1,2},{2,3},{3,4},{4,5},{5,6},{6,7},{15,8},{8,9},{9,10... | collective-permute-start | bytes 589832 | tf_op jit(solution)/shard_map/while/body/eval_jaxpr/ppermute | solution.py:28
  283.7 8.2 %collective-permute-start = (bf16[64,1536]{1,0:T(8,128)(2,1)S(1)}, bf16[64,1536]{1,0:T(8,128)(2,1)S(1)}, u32[]{:S(2)}, u32[]{:S(2)}) collective-permute-start(bf16[64,1536]{1,0:T(8,128)(2,1)S(1)} %get-tuple-element.648), channel_id=1, source_target_pairs={{7,0},{0,1},{1,2},{2,3},{3,4},{4,5},{5,6},{6,7},{15,8},{8,9},{9,10... | collective-permute-start | bytes 589832 | tf_op jit(solution)/shard_map/while/body/eval_jaxpr/ppermute | solution.py:28
  294.2 8.2 %collective-permute-start = (bf16[64,1536]{1,0:T(8,128)(2,1)S(1)}, bf16[64,1536]{1,0:T(8,128)(2,1)S(1)}, u32[]{:S(2)}, u32[]{:S(2)}) collective-permute-start(bf16[64,1536]{1,0:T(8,128)(2,1)S(1)} %get-tuple-element.648), channel_id=1, source_target_pairs={{7,0},{0,1},{1,2},{2,3},{3,4},{4,5},{5,6},{6,7},{15,8},{8,9},{9,10... | collective-permute-start | bytes 589832 | tf_op jit(solution)/shard_map/while/body/eval_jaxpr/ppermute | solution.py:28
  304.7 14.0 %collective-permute-start = (bf16[64,1536]{1,0:T(8,128)(2,1)S(1)}, bf16[64,1536]{1,0:T(8,128)(2,1)S(1)}, u32[]{:S(2)}, u32[]{:S(2)}) collective-permute-start(bf16[64,1536]{1,0:T(8,128)(2,1)S(1)} %get-tuple-element.648), channel_id=1, source_target_pairs={{7,0},{0,1},{1,2},{2,3},{3,4},{4,5},{5,6},{6,7},{15,8},{8,9},{9,10... | collective-permute-start | bytes 589832 | tf_op jit(solution)/shard_map/while/body/eval_jaxpr/ppermute | solution.py:28
  320.9 13.1 %collective-permute-start = (bf16[64,1536]{1,0:T(8,128)(2,1)S(1)}, bf16[64,1536]{1,0:T(8,128)(2,1)S(1)}, u32[]{:S(2)}, u32[]{:S(2)}) collective-permute-start(bf16[64,1536]{1,0:T(8,128)(2,1)S(1)} %get-tuple-element.648), channel_id=1, source_target_pairs={{7,0},{0,1},{1,2},{2,3},{3,4},{4,5},{5,6},{6,7},{15,8},{8,9},{9,10... | collective-permute-start | bytes 589832 | tf_op jit(solution)/shard_map/while/body/eval_jaxpr/ppermute | solution.py:28
  336.4 12.0 %collective-permute-start = (bf16[64,1536]{1,0:T(8,128)(2,1)S(1)}, bf16[64,1536]{1,0:T(8,128)(2,1)S(1)}, u32[]{:S(2)}, u32[]{:S(2)}) collective-permute-start(bf16[64,1536]{1,0:T(8,128)(2,1)S(1)} %get-tuple-element.648), channel_id=1, source_target_pairs={{7,0},{0,1},{1,2},{2,3},{3,4},{4,5},{5,6},{6,7},{15,8},{8,9},{9,10... | collective-permute-start | bytes 589832 | tf_op jit(solution)/shard_map/while/body/eval_jaxpr/ppermute | solution.py:28
  349.2 1.3 copy-start.7
  351.4 45.6 %all-to-all-start.1 = ((bf16[32,48,192]{2,1,0:T(8,128)(2,1)}), bf16[32,48,192]{2,1,0:T(8,128)(2,1)S(1)}, u32[]{:S(2)}, u32[]{:S(2)}) async-start(bf16[32,48,192]{2,1,0:T(8,128)(2,1)} %broadcast_in_dim.73), calls=%async_computation.1 | async-start | bytes 1572864 | tf_op jit(solution)/shard_map/all_to_all | solution.py:43
  375.8 1.3 copy-start.9
  381.7 15.8 %copy-start.4 = (bf16[192,512]{1,0:T(8,128)(2,1)S(1)}, bf16[192,512]{1,0:T(8,128)(2,1)}, u32[]{:S(2)}) copy-start(bf16[192,512]{1,0:T(8,128)(2,1)} %param.27) | copy-start | bytes 589828
  397.9 67.9 %copy-start.5 = (bf16[192,512]{1,0:T(8,128)(2,1)S(1)}, bf16[192,512]{1,0:T(8,128)(2,1)}, u32[]{:S(2)}) copy-start(bf16[192,512]{1,0:T(8,128)(2,1)} %param.27) | copy-start | bytes 589828
  465.7 15.3 %copy-start.3 = (bf16[4,64,1536]{2,1,0:T(8,128)(2,1)}, bf16[4,64,1536]{2,1,0:T(8,128)(2,1)S(1)}, u32[]{:S(2)}) copy-start(bf16[4,64,1536]{2,1,0:T(8,128)(2,1)S(1)} %slice.46) | copy-start | bytes 2359300
  465.7 4.7 copy-start.12
  466.0 15.1 %copy-start.10 = (f32[512]{0:T(512)S(1)}, f32[512]{0:T(512)}, u32[]{:S(2)}) copy-start(f32[512]{0:T(512)} %param.28) | copy-start | bytes 6148
  466.9 14.0 %all-to-all-start.2 = ((bf16[8,32,1024]{2,1,0:T(8,128)(2,1)}), bf16[8,32,1024]{2,1,0:T(8,128)(2,1)S(1)}, u32[]{:S(2)}, u32[]{:S(2)}) async-start(bf16[8,32,1024]{2,1,0:T(8,128)(2,1)} %bitcast.17), calls=%async_computation.2 | async-start | bytes 1048576 | tf_op jit(solution)/shard_map/all_to_all | solution.py:52
Sparse Core Ops, SparseCore 0:
  9.9 80.5 all-gather.3
  350.6 113.7 all-gather.5
where the time goes:
time: 553 us; the launch traced here: 551 us
  waiting for transfers between devices  296 us (54%)
  starting transfers between devices  59.4 us (11%)
  blocking collectives  58.4 us (11%)
  other arithmetic  50.8 us (9%)
  local copies, waits for them, and re-layouts  36.1 us (7%)
  matrix products  32.4 us (6%)
  between operations  14.5 us (3%)
    ppermute x19, waiting for transfers between devices, from_behind(): return lax.ppermute(block, axis, route)  152 us
    all_gather x1, waiting for transfers between devices, picked(): lax.all_gather(x, axis)  66.6 us
    all_to_all x3, blocking collectives, from_everyone(): return lax.all_to_all(copies, axis, split_axis=0, concat_axis=0, tiled=True)  33.7 us
    dot_general x8, matrix products, teacher_block(): mixed = jnp.dot(inputs, weight, preferred_element_type=jnp.float32)  27.2 us
    all_to_all x1, waiting for transfers between devices, summed_on_arrival(): lax.all_to_all(blocks, axis, split_axis=0, concat_axis=0, tiled=True)  26.8 us
    all_gather x1, waiting for transfers between devices, local(): weights = lax.all_gather(block_weight, DP, axis=1, tiled=True)[0]  24.6 us
    all_to_all x1, starting transfers between devices, from_everyone(): return lax.all_to_all(copies, axis, split_axis=0, concat_axis=0, tiled=True)  24.4 us
    ppermute x19, starting transfers between devices, from_behind(): return lax.ppermute(block, axis, route)  20.4 us
  transfers between devices with their start and end apart: 24, of which 24 were waited for; matrix products, arithmetic and copies ran while one was open for 5% of the time, Pallas kernels for 0%

commit v1 on v0

--- a/solution.py
+++ b/solution.py
@@ -154,7 +154,9 @@
         DP,
         0,
     )
-    weights = lax.all_gather(block_weight, DP, axis=1, tiled=True)[0]
+    weights = jnp.concatenate(
+        lax.all_to_all(jnp.stack([block_weight] * lax.axis_size(DP)), DP, 0, 0), axis=1
+    )[0]
     section_mod = block_mod[0]
     indices_f = sched_index.astype(jnp.float32)
     half_freq = time_weight.shape[0] // 2

time: 553 us -> 635 us (1.15)
  waiting for transfers between devices: 296 us -> 350 us
  blocking collectives: 58.4 us -> 90.6 us
  starting transfers between devices: 59.4 us -> 52.2 us
    all_to_all x1, waiting for transfers between devices: 26.8 us -> 102 us  [local(): lax.all_to_all(jnp.stack([block_weight] * lax.axis_size(DP)), DP, 0, 0)]
    all_to_all x0 -> x1, blocking collectives: none -> 32.2 us  [summed_on_arrival(): lax.all_to_all(blocks, axis, split_axis=0, concat_axis=0, tiled=True)]
    all_gather x1 -> x0, waiting for transfers between devices: 24.6 us -> none  [local(): weights = lax.all_gather(block_weight, DP, axis=1, tiled=True)[0]]
  transfers between devices with their start and end apart: 24 -> 23, of which waited for: 24 -> 23; matrix products, arithmetic and copies ran while one was open for 5% -> 2% of each run, Pallas kernels for 0% -> 0%
where the time goes in v1:
time: 635 us; the launch traced here: 632 us
  waiting for transfers between devices  350 us (55%)
  blocking collectives  90.6 us (14%)
  starting transfers between devices  52.2 us (8%)
  other arithmetic  51.6 us (8%)
  local copies, waits for them, and re-layouts  38.2 us (6%)
  matrix products  32.4 us (5%)
  between operations  14.5 us (2%)
    ppermute x19, waiting for transfers between devices, from_behind(): return lax.ppermute(block, axis, route)  156 us
    all_to_all x1, waiting for transfers between devices, local(): lax.all_to_all(jnp.stack([block_weight] * lax.axis_size(DP)), DP, 0, 0)  102 us
    all_gather x1, waiting for transfers between devices, picked(): lax.all_gather(x, axis)  66.6 us
    all_to_all x3, blocking collectives, from_everyone(): return lax.all_to_all(copies, axis, split_axis=0, concat_axis=0, tiled=True)  33.7 us
    all_to_all x1, blocking collectives, summed_on_arrival(): lax.all_to_all(blocks, axis, split_axis=0, concat_axis=0, tiled=True)  32.2 us
    dot_general x8, matrix products, teacher_block(): mixed = jnp.dot(inputs, weight, preferred_element_type=jnp.float32)  27.2 us
    all_to_all x1, starting transfers between devices, from_everyone(): return lax.all_to_all(copies, axis, split_axis=0, concat_axis=0, tiled=True)  24 us
    all_to_all x1, blocking collectives, summed_rows(): lax.all_to_all(own.astype(jnp.bfloat16), far, 0, 0, tiled=True)  17.7 us
  transfers between devices with their start and end apart: 23, of which 23 were waited for; matrix products, arithmetic and copies ran while one was open for 2% of the time, Pallas kernels for 0%

profile of v1, /device:TPU:1, one launch (start us, length us, event | category | flops | bytes accessed | tf_op | source)
XLA Modules:
  0.0 632.4 jit_solution(9712491576433756895)
XLA Ops:
  8.1 10.4 %while.33 = (s32[]{:T(128)}, f32[128,1544]{0,1:T(8,128)S(1)}, s32[128,77]{0,1:T(8,128)S(1)}, s32[]{:T(128)}, s32[]{:T(128)}, /*index=5*/s32[]{:T(128)}, s32[]{:T(128)}) while((s32[]{:T(128)}, f32[128,1544]{0,1:T(8,128)S(1)}, s32[128,77]{0,1:T(8,128)S(1)}, s32[]{:T(128)}, s32[]{:T(128)}, /*index=5*/s32[]{:T(128)}, s32[]{:T(128)}) %tuple.112), condition=%wide.region_2.0_spmd.clone, body=%wide.region_0.0_spmd.clone.sunk | while | flops 4347911 | bytes 3173001 | solution.py:145
  22.0 32.2 %all_to_all.45 = f32[32,4,1536]{2,1,0:T(4,128)} all-to-all(f32[32,4,1536]{2,1,0:T(4,128)S(1)} %reshape.124), channel_id=1, replica_groups=mesh['dp_0'=2,'dp_1'=8,'dp_2'=2,'section'=8] {'dp_0','dp_1','dp_2'}, dimensions={0} | all-to-all | bytes 1572864 | tf_op jit(solution)/shard_map/all_to_all | solution.py:21
  56.9 6.9 %all-to-all-start.1 = ((bf16[32,1,48,1536]{3,2,1,0:T(8,128)(2,1)}), bf16[32,1,48,1536]{3,2,1,0:T(8,128)(2,1)}, u32[]{:S(2)}, u32[]{:S(2)}) async-start(bf16[32,1,48,1536]{3,2,1,0:T(8,128)(2,1)} %stack.2), calls=%async_computation.1 | async-start | bytes 9437184 | tf_op jit(solution)/shard_map/all_to_all | solution.py:158
  68.3 101.5 %all-to-all-done.1 = bf16[32,1,48,1536]{3,2,1,0:T(8,128)(2,1)} async-done(((bf16[32,1,48,1536]{3,2,1,0:T(8,128)(2,1)}), bf16[32,1,48,1536]{3,2,1,0:T(8,128)(2,1)}, u32[]{:S(2)}, u32[]{:S(2)}) %all-to-all-start.1) | async-done | bytes 4718624 | tf_op jit(solution)/shard_map/all_to_all | solution.py:158
  169.8 261.7 %while.32 = (s32[]{:T(128)}, bf16[4,64,1536]{2,1,0:T(8,128)(2,1)S(1)}, bf16[4,64,1536]{2,1,0:T(8,128)(2,1)S(1)}, s32[]{:T(128)}, s32[]{:T(128)}, /*index=5*/pred...) while((s32[]{:T(128)}, ...), condition=%wide.region_8.9_spmd, body=%wide.region_4.8_spmd.sunk | while | flops 305340000 | bytes 8762968 | solution.py:216
  171.2 5.3 conditional.2
  176.7 8.9 %collective-permute-done = bf16[64,1536]{1,0:T(8,128)(2,1)S(1)} collective-permute-done((bf16[64,1536]{1,0:T(8,128)(2,1)S(1)}, bf16[64,1536]{1,0:T(8,128)(2,1)S(1)}, u32[]{:S(2)}, u32[]{:S(2)}) %collective-permute-start) | collective-permute-done | bytes 196640 | tf_op jit(solution)/shard_map/while/body/eval_jaxpr/ppermute | solution.py:28
  187.8 5.3 conditional.2
  189.7 3.4 fusion.6
  193.3 8.1 %collective-permute-done = bf16[64,1536]{1,0:T(8,128)(2,1)S(1)} collective-permute-done((bf16[64,1536]{1,0:T(8,128)(2,1)S(1)}, bf16[64,1536]{1,0:T(8,128)(2,1)S(1)}, u32[]{:S(2)}, u32[]{:S(2)}) %collective-permute-start) | collective-permute-done | bytes 196640 | tf_op jit(solution)/shard_map/while/body/eval_jaxpr/ppermute | solution.py:28
  203.7 5.3 conditional.2
  205.6 3.4 fusion.6
  209.1 8.1 %collective-permute-done = bf16[64,1536]{1,0:T(8,128)(2,1)S(1)} collective-permute-done((bf16[64,1536]{1,0:T(8,128)(2,1)S(1)}, bf16[64,1536]{1,0:T(8,128)(2,1)S(1)}, u32[]{:S(2)}, u32[]{:S(2)}) %collective-permute-start) | collective-permute-done | bytes 196640 | tf_op jit(solution)/shard_map/while/body/eval_jaxpr/ppermute | solution.py:28
  219.5 5.3 conditional.2
  221.4 3.4 fusion.6
  225.0 8.1 %collective-permute-done = bf16[64,1536]{1,0:T(8,128)(2,1)S(1)} collective-permute-done((bf16[64,1536]{1,0:T(8,128)(2,1)S(1)}, bf16[64,1536]{1,0:T(8,128)(2,1)S(1)}, u32[]{:S(2)}, u32[]{:S(2)}) %collective-permute-start) | collective-permute-done | bytes 196640 | tf_op jit(solution)/shard_map/while/body/eval_jaxpr/ppermute | solution.py:28
  238.6 4.9 collective-permute-done
  247.1 7.1 %collective-permute-done = bf16[64,1536]{1,0:T(8,128)(2,1)S(1)} collective-permute-done((bf16[64,1536]{1,0:T(8,128)(2,1)S(1)}, bf16[64,1536]{1,0:T(8,128)(2,1)S(1)}, u32[]{:S(2)}, u32[]{:S(2)}) %collective-permute-start) | collective-permute-done | bytes 196640 | tf_op jit(solution)/shard_map/while/body/eval_jaxpr/ppermute | solution.py:28
  258.3 6.4 %collective-permute-done = bf16[64,1536]{1,0:T(8,128)(2,1)S(1)} collective-permute-done((bf16[64,1536]{1,0:T(8,128)(2,1)S(1)}, bf16[64,1536]{1,0:T(8,128)(2,1)S(1)}, u32[]{:S(2)}, u32[]{:S(2)}) %collective-permute-start) | collective-permute-done | bytes 196640 | tf_op jit(solution)/shard_map/while/body/eval_jaxpr/ppermute | solution.py:28
  267.6 7.6 %collective-permute-done = bf16[64,1536]{1,0:T(8,128)(2,1)S(1)} collective-permute-done((bf16[64,1536]{1,0:T(8,128)(2,1)S(1)}, bf16[64,1536]{1,0:T(8,128)(2,1)S(1)}, u32[]{:S(2)}, u32[]{:S(2)}) %collective-permute-start) | collective-permute-done | bytes 196640 | tf_op jit(solution)/shard_map/while/body/eval_jaxpr/ppermute | solution.py:28
  277.6 5.3 conditional.2
  283.0 8.1 %collective-permute-done = bf16[64,1536]{1,0:T(8,128)(2,1)S(1)} collective-permute-done((bf16[64,1536]{1,0:T(8,128)(2,1)S(1)}, bf16[64,1536]{1,0:T(8,128)(2,1)S(1)}, u32[]{:S(2)}, u32[]{:S(2)}) %collective-permute-start) | collective-permute-done | bytes 196640 | tf_op jit(solution)/shard_map/while/body/eval_jaxpr/ppermute | solution.py:28
  293.4 5.3 conditional.2
  295.3 3.4 fusion.6
  298.8 8.1 %collective-permute-done = bf16[64,1536]{1,0:T(8,128)(2,1)S(1)} collective-permute-done((bf16[64,1536]{1,0:T(8,128)(2,1)S(1)}, bf16[64,1536]{1,0:T(8,128)(2,1)S(1)}, u32[]{:S(2)}, u32[]{:S(2)}) %collective-permute-start) | collective-permute-done | bytes 196640 | tf_op jit(solution)/shard_map/while/body/eval_jaxpr/ppermute | solution.py:28
  309.2 5.3 conditional.2
  311.1 3.4 fusion.6
  314.7 8.1 %collective-permute-done = bf16[64,1536]{1,0:T(8,128)(2,1)S(1)} collective-permute-done((bf16[64,1536]{1,0:T(8,128)(2,1)S(1)}, bf16[64,1536]{1,0:T(8,128)(2,1)S(1)}, u32[]{:S(2)}, u32[]{:S(2)}) %collective-permute-start) | collective-permute-done | bytes 196640 | tf_op jit(solution)/shard_map/while/body/eval_jaxpr/ppermute | solution.py:28
  325.0 5.3 conditional.2
  326.9 3.4 fusion.6
  330.5 8.1 %collective-permute-done = bf16[64,1536]{1,0:T(8,128)(2,1)S(1)} collective-permute-done((bf16[64,1536]{1,0:T(8,128)(2,1)S(1)}, bf16[64,1536]{1,0:T(8,128)(2,1)S(1)}, u32[]{:S(2)}, u32[]{:S(2)}) %collective-permute-start) | collective-permute-done | bytes 196640 | tf_op jit(solution)/shard_map/while/body/eval_jaxpr/ppermute | solution.py:28
  344.2 4.9 collective-permute-done
  354.9 4.8 collective-permute-done
  363.8 6.4 %collective-permute-done = bf16[64,1536]{1,0:T(8,128)(2,1)S(1)} collective-permute-done((bf16[64,1536]{1,0:T(8,128)(2,1)S(1)}, bf16[64,1536]{1,0:T(8,128)(2,1)S(1)}, u32[]{:S(2)}, u32[]{:S(2)}) %collective-permute-start) | collective-permute-done | bytes 196640 | tf_op jit(solution)/shard_map/while/body/eval_jaxpr/ppermute | solution.py:28
  373.6 7.2 %collective-permute-done = bf16[64,1536]{1,0:T(8,128)(2,1)S(1)} collective-permute-done((bf16[64,1536]{1,0:T(8,128)(2,1)S(1)}, bf16[64,1536]{1,0:T(8,128)(2,1)S(1)}, u32[]{:S(2)}, u32[]{:S(2)}) %collective-permute-start) | collective-permute-done | bytes 196640 | tf_op jit(solution)/shard_map/while/body/eval_jaxpr/ppermute | solution.py:28
  383.8 12.8 %collective-permute-done = bf16[64,1536]{1,0:T(8,128)(2,1)S(1)} collective-permute-done((bf16[64,1536]{1,0:T(8,128)(2,1)S(1)}, bf16[64,1536]{1,0:T(8,128)(2,1)S(1)}, u32[]{:S(2)}, u32[]{:S(2)}) %collective-permute-start) | collective-permute-done | bytes 196640 | tf_op jit(solution)/shard_map/while/body/eval_jaxpr/ppermute | solution.py:28
  399.0 12.8 %collective-permute-done = bf16[64,1536]{1,0:T(8,128)(2,1)S(1)} collective-permute-done((bf16[64,1536]{1,0:T(8,128)(2,1)S(1)}, bf16[64,1536]{1,0:T(8,128)(2,1)S(1)}, u32[]{:S(2)}, u32[]{:S(2)}) %collective-permute-start) | collective-permute-done | bytes 196640 | tf_op jit(solution)/shard_map/while/body/eval_jaxpr/ppermute | solution.py:28
  414.3 16.3 %collective-permute-done = bf16[64,1536]{1,0:T(8,128)(2,1)S(1)} collective-permute-done((bf16[64,1536]{1,0:T(8,128)(2,1)S(1)}, bf16[64,1536]{1,0:T(8,128)(2,1)S(1)}, u32[]{:S(2)}, u32[]{:S(2)}) %collective-permute-start) | collective-permute-done | bytes 196640 | tf_op jit(solution)/shard_map/while/body/eval_jaxpr/ppermute | solution.py:28
  433.7 24.0 %all-to-all-start.2 = ((bf16[32,48,192]{2,1,0:T(8,128)(2,1)}), bf16[32,48,192]{2,1,0:T(8,128)(2,1)S(1)}, u32[]{:S(2)}, u32[]{:S(2)}) async-start(bf16[32,48,192]{2,1,0:T(8,128)(2,1)} %broadcast_in_dim.73), calls=%async_computation.2 | async-start | bytes 1572864 | tf_op jit(solution)/shard_map/all_to_all | solution.py:43
  463.6 15.4 %all-to-all-done.2 = bf16[32,48,192]{2,1,0:T(8,128)(2,1)S(1)} async-done(((bf16[32,48,192]{2,1,0:T(8,128)(2,1)}), bf16[32,48,192]{2,1,0:T(8,128)(2,1)S(1)}, u32[]{:S(2)}, u32[]{:S(2)}) %all-to-all-start.2) | async-done | bytes 589856 | tf_op jit(solution)/shard_map/all_to_all | solution.py:43
  479.8 66.6 %all-gather.3.cloned.1.call-done = bf16[32,64,1536]{2,1,0:T(8,128)(2,1)} async-done(((bf16[4,64,1536]{2,1,0:T(8,128)(2,1)}), bf16[32,64,1536]{2,1,0:T(8,128)(2,1)}) %all-gather.3.cloned.1.call-update) | async-done | bytes 6291472 | tf_op jit(solution)/shard_map/all_gather | solution.py:32
  548.8 3.5 all-to-all-start.3
  552.4 10.4 %all-to-all-done.3 = bf16[8,32,1024]{2,1,0:T(8,128)(2,1)S(1)} async-done(((bf16[8,32,1024]{2,1,0:T(8,128)(2,1)}), bf16[8,32,1024]{2,1,0:T(8,128)(2,1)S(1)}, u32[]{:S(2)}, u32[]{:S(2)}) %all-to-all-start.3) | async-done | bytes 524320 | tf_op jit(solution)/shard_map/all_to_all | solution.py:52
  563.8 10.3 %all_to_all.46 = bf16[8,32,512]{2,1,0:T(8,128)(2,1)S(1)} all-to-all(bf16[8,32,512]{2,1,0:T(8,128)(2,1)S(1)} %broadcast_in_dim.76), channel_id=1, replica_groups=mesh['dp_0'=2,'dp_1'=8,'dp_2'=2,'section'=8] {'section'}, dimensions={0} | all-to-all | bytes 524288 | tf_op jit(solution)/shard_map/all_to_all | solution.py:43
  575.2 7.0 %all_to_all.47 = bf16[2,16,48,192]{3,2,1,0:T(8,128)(2,1)S(1)} all-to-all(bf16[2,16,48,192]{3,2,1,0:T(8,128)(2,1)S(1)} %copy.46), channel_id=1, replica_groups=mesh['dp_0'=2,'dp_1'=8,'dp_2'=2,'section'=8] {'dp_2'}, dimensions={0} | all-to-all | bytes 1179648 | tf_op jit(solution)/shard_map/all_to_all | solution.py:52
  582.5 17.7 %all_to_all.48 = bf16[16,48,192]{2,1,0:T(8,128)(2,1)S(1)} all-to-all(bf16[16,48,192]{2,1,0:T(8,128)(2,1)S(1)} %reduce_sum.120), channel_id=1, replica_groups=mesh['dp_0'=2,'dp_1'=8,'dp_2'=2,'section'=8] {'dp_0','dp_1'}, dimensions={0} | all-to-all | bytes 589824 | tf_op jit(solution)/shard_map/all_to_all | solution.py:79
  600.3 16.9 %all_to_all.49 = bf16[16,48,192]{2,1,0:T(8,128)(2,1)S(1)} all-to-all(bf16[16,48,192]{2,1,0:T(8,128)(2,1)S(1)} %broadcast_in_dim.77), channel_id=1, replica_groups=mesh['dp_0'=2,'dp_1'=8,'dp_2'=2,'section'=8] {'dp_0','dp_1'}, dimensions={0} | all-to-all | bytes 589824 | tf_op jit(solution)/shard_map/all_to_all | solution.py:43
  617.3 6.4 %all_to_all.50 = bf16[2,16,48,192]{3,2,1,0:T(8,128)(2,1)S(1)} all-to-all(bf16[2,16,48,192]{3,2,1,0:T(8,128)(2,1)S(1)} %broadcast_in_dim.78), channel_id=1, replica_groups=mesh['dp_0'=2,'dp_1'=8,'dp_2'=2,'section'=8] {'dp_2'}, dimensions={0} | all-to-all | bytes 1179648 | tf_op jit(solution)/shard_map/all_to_all | solution.py:43
  (276 shorter events, 119.6 us)
Async XLA Ops:
  7.2 59.5 %copy-start = (bf16[256,1536]{1,0:T(8,128)(2,1)S(1)}, bf16[256,1536]{1,0:T(8,128)(2,1)}, u32[]{:S(2)}) copy-start(bf16[256,1536]{1,0:T(8,128)(2,1)} %param.22) | copy-start | bytes 2359300
  21.7 32.5 %copy-start.6 = (bf16[1,48,1536]{2,1,0:T(8,128)(2,1)S(1)}, bf16[1,48,1536]{2,1,0:T(8,128)(2,1)}, u32[]{:S(2)}) copy-start(bf16[1,48,1536]{2,1,0:T(8,128)(2,1)} %param.23) | copy-start | bytes 442372
  56.9 7.0 %copy-start.1 = (bf16[4,64,1536]{2,1,0:T(8,128)(2,1)S(1)}, bf16[4,64,1536]{2,1,0:T(8,128)(2,1)}, u32[]{:S(2)}) copy-start(bf16[4,64,1536]{2,1,0:T(8,128)(2,1)} %param.18) | copy-start | bytes 2359300
  56.9 112.9 %all-to-all-start.1 = ((bf16[32,1,48,1536]{3,2,1,0:T(8,128)(2,1)}), bf16[32,1,48,1536]{3,2,1,0:T(8,128)(2,1)}, u32[]{:S(2)}, u32[]{:S(2)}) async-start(bf16[32,1,48,1536]{3,2,1,0:T(8,128)(2,1)} %stack.2), calls=%async_computation.1 | async-start | bytes 9437184 | tf_op jit(solution)/shard_map/all_to_all | solution.py:158
  63.8 482.6 %all-gather.3.cloned.1.call-start = ((), (), s32[]{:S(2)}) async-start(), calls=%async_computation.9 | async-start | bytes 7077888 | tf_op jit(solution)/shard_map/all_gather | solution.py:32
  63.9 0.7 copy-start.12
  63.9 0.8 copy-start.9
  64.0 105.8 %copy-start.2 = (bf16[4,64,1536]{2,1,0:T(8,128)(2,1)S(1)}, bf16[4,64,1536]{2,1,0:T(8,128)(2,1)}, u32[]{:S(2)}) copy-start(bf16[4,64,1536]{2,1,0:T(8,128)(2,1)} %param.18) | copy-start | bytes 2359300
  66.9 0.6 copy-start.7
  176.5 9.0 %collective-permute-start = (bf16[64,1536]{1,0:T(8,128)(2,1)S(1)}, bf16[64,1536]{1,0:T(8,128)(2,1)S(1)}, u32[]{:S(2)}, u32[]{:S(2)}) collective-permute-start(bf16[64,1536]{1,0:T(8,128)(2,1)S(1)} %get-tuple-element.648), channel_id=1, source_target_pairs={{7,0},{0,1},{1,2},{2,3},{3,4},{4,5},{5,6},{6,7},{15,8},{8,9},{9,10... | collective-permute-start | bytes 589832 | tf_op jit(solution)/shard_map/while/body/eval_jaxpr/ppermute | solution.py:28
  193.1 8.2 %collective-permute-start = (bf16[64,1536]{1,0:T(8,128)(2,1)S(1)}, bf16[64,1536]{1,0:T(8,128)(2,1)S(1)}, u32[]{:S(2)}, u32[]{:S(2)}) collective-permute-start(bf16[64,1536]{1,0:T(8,128)(2,1)S(1)} %get-tuple-element.648), channel_id=1, source_target_pairs={{7,0},{0,1},{1,2},{2,3},{3,4},{4,5},{5,6},{6,7},{15,8},{8,9},{9,10... | collective-permute-start | bytes 589832 | tf_op jit(solution)/shard_map/while/body/eval_jaxpr/ppermute | solution.py:28
  209.0 8.2 %collective-permute-start = (bf16[64,1536]{1,0:T(8,128)(2,1)S(1)}, bf16[64,1536]{1,0:T(8,128)(2,1)S(1)}, u32[]{:S(2)}, u32[]{:S(2)}) collective-permute-start(bf16[64,1536]{1,0:T(8,128)(2,1)S(1)} %get-tuple-element.648), channel_id=1, source_target_pairs={{7,0},{0,1},{1,2},{2,3},{3,4},{4,5},{5,6},{6,7},{15,8},{8,9},{9,10... | collective-permute-start | bytes 589832 | tf_op jit(solution)/shard_map/while/body/eval_jaxpr/ppermute | solution.py:28
  224.8 8.2 %collective-permute-start = (bf16[64,1536]{1,0:T(8,128)(2,1)S(1)}, bf16[64,1536]{1,0:T(8,128)(2,1)S(1)}, u32[]{:S(2)}, u32[]{:S(2)}) collective-permute-start(bf16[64,1536]{1,0:T(8,128)(2,1)S(1)} %get-tuple-element.648), channel_id=1, source_target_pairs={{7,0},{0,1},{1,2},{2,3},{3,4},{4,5},{5,6},{6,7},{15,8},{8,9},{9,10... | collective-permute-start | bytes 589832 | tf_op jit(solution)/shard_map/while/body/eval_jaxpr/ppermute | solution.py:28
  235.4 8.2 %collective-permute-start = (bf16[64,1536]{1,0:T(8,128)(2,1)S(1)}, bf16[64,1536]{1,0:T(8,128)(2,1)S(1)}, u32[]{:S(2)}, u32[]{:S(2)}) collective-permute-start(bf16[64,1536]{1,0:T(8,128)(2,1)S(1)} %get-tuple-element.648), channel_id=1, source_target_pairs={{7,0},{0,1},{1,2},{2,3},{3,4},{4,5},{5,6},{6,7},{15,8},{8,9},{9,10... | collective-permute-start | bytes 589832 | tf_op jit(solution)/shard_map/while/body/eval_jaxpr/ppermute | solution.py:28
  245.9 8.2 %collective-permute-start = (bf16[64,1536]{1,0:T(8,128)(2,1)S(1)}, bf16[64,1536]{1,0:T(8,128)(2,1)S(1)}, u32[]{:S(2)}, u32[]{:S(2)}) collective-permute-start(bf16[64,1536]{1,0:T(8,128)(2,1)S(1)} %get-tuple-element.648), channel_id=1, source_target_pairs={{7,0},{0,1},{1,2},{2,3},{3,4},{4,5},{5,6},{6,7},{15,8},{8,9},{9,10... | collective-permute-start | bytes 589832 | tf_op jit(solution)/shard_map/while/body/eval_jaxpr/ppermute | solution.py:28
  256.5 8.2 %collective-permute-start = (bf16[64,1536]{1,0:T(8,128)(2,1)S(1)}, bf16[64,1536]{1,0:T(8,128)(2,1)S(1)}, u32[]{:S(2)}, u32[]{:S(2)}) collective-permute-start(bf16[64,1536]{1,0:T(8,128)(2,1)S(1)} %get-tuple-element.648), channel_id=1, source_target_pairs={{7,0},{0,1},{1,2},{2,3},{3,4},{4,5},{5,6},{6,7},{15,8},{8,9},{9,10... | collective-permute-start | bytes 589832 | tf_op jit(solution)/shard_map/while/body/eval_jaxpr/ppermute | solution.py:28
  267.0 8.2 %collective-permute-start = (bf16[64,1536]{1,0:T(8,128)(2,1)S(1)}, bf16[64,1536]{1,0:T(8,128)(2,1)S(1)}, u32[]{:S(2)}, u32[]{:S(2)}) collective-permute-start(bf16[64,1536]{1,0:T(8,128)(2,1)S(1)} %get-tuple-element.648), channel_id=1, source_target_pairs={{7,0},{0,1},{1,2},{2,3},{3,4},{4,5},{5,6},{6,7},{15,8},{8,9},{9,10... | collective-permute-start | bytes 589832 | tf_op jit(solution)/shard_map/while/body/eval_jaxpr/ppermute | solution.py:28
  282.8 8.2 %collective-permute-start = (bf16[64,1536]{1,0:T(8,128)(2,1)S(1)}, bf16[64,1536]{1,0:T(8,128)(2,1)S(1)}, u32[]{:S(2)}, u32[]{:S(2)}) collective-permute-start(bf16[64,1536]{1,0:T(8,128)(2,1)S(1)} %get-tuple-element.648), channel_id=1, source_target_pairs={{7,0},{0,1},{1,2},{2,3},{3,4},{4,5},{5,6},{6,7},{15,8},{8,9},{9,10... | collective-permute-start | bytes 589832 | tf_op jit(solution)/shard_map/while/body/eval_jaxpr/ppermute | solution.py:28
  298.7 8.2 %collective-permute-start = (bf16[64,1536]{1,0:T(8,128)(2,1)S(1)}, bf16[64,1536]{1,0:T(8,128)(2,1)S(1)}, u32[]{:S(2)}, u32[]{:S(2)}) collective-permute-start(bf16[64,1536]{1,0:T(8,128)(2,1)S(1)} %get-tuple-element.648), channel_id=1, source_target_pairs={{7,0},{0,1},{1,2},{2,3},{3,4},{4,5},{5,6},{6,7},{15,8},{8,9},{9,10... | collective-permute-start | bytes 589832 | tf_op jit(solution)/shard_map/while/body/eval_jaxpr/ppermute | solution.py:28
  314.5 8.2 %collective-permute-start = (bf16[64,1536]{1,0:T(8,128)(2,1)S(1)}, bf16[64,1536]{1,0:T(8,128)(2,1)S(1)}, u32[]{:S(2)}, u32[]{:S(2)}) collective-permute-start(bf16[64,1536]{1,0:T(8,128)(2,1)S(1)} %get-tuple-element.648), channel_id=1, source_target_pairs={{7,0},{0,1},{1,2},{2,3},{3,4},{4,5},{5,6},{6,7},{15,8},{8,9},{9,10... | collective-permute-start | bytes 589832 | tf_op jit(solution)/shard_map/while/body/eval_jaxpr/ppermute | solution.py:28
  330.3 8.2 %collective-permute-start = (bf16[64,1536]{1,0:T(8,128)(2,1)S(1)}, bf16[64,1536]{1,0:T(8,128)(2,1)S(1)}, u32[]{:S(2)}, u32[]{:S(2)}) collective-permute-start(bf16[64,1536]{1,0:T(8,128)(2,1)S(1)} %get-tuple-element.648), channel_id=1, source_target_pairs={{7,0},{0,1},{1,2},{2,3},{3,4},{4,5},{5,6},{6,7},{15,8},{8,9},{9,10... | collective-permute-start | bytes 589832 | tf_op jit(solution)/shard_map/while/body/eval_jaxpr/ppermute | solution.py:28
  340.9 8.2 %collective-permute-start = (bf16[64,1536]{1,0:T(8,128)(2,1)S(1)}, bf16[64,1536]{1,0:T(8,128)(2,1)S(1)}, u32[]{:S(2)}, u32[]{:S(2)}) collective-permute-start(bf16[64,1536]{1,0:T(8,128)(2,1)S(1)} %get-tuple-element.648), channel_id=1, source_target_pairs={{7,0},{0,1},{1,2},{2,3},{3,4},{4,5},{5,6},{6,7},{15,8},{8,9},{9,10... | collective-permute-start | bytes 589832 | tf_op jit(solution)/shard_map/while/body/eval_jaxpr/ppermute | solution.py:28
  351.4 8.2 %collective-permute-start = (bf16[64,1536]{1,0:T(8,128)(2,1)S(1)}, bf16[64,1536]{1,0:T(8,128)(2,1)S(1)}, u32[]{:S(2)}, u32[]{:S(2)}) collective-permute-start(bf16[64,1536]{1,0:T(8,128)(2,1)S(1)} %get-tuple-element.648), channel_id=1, source_target_pairs={{7,0},{0,1},{1,2},{2,3},{3,4},{4,5},{5,6},{6,7},{15,8},{8,9},{9,10... | collective-permute-start | bytes 589832 | tf_op jit(solution)/shard_map/while/body/eval_jaxpr/ppermute | solution.py:28
  362.0 8.2 %collective-permute-start = (bf16[64,1536]{1,0:T(8,128)(2,1)S(1)}, bf16[64,1536]{1,0:T(8,128)(2,1)S(1)}, u32[]{:S(2)}, u32[]{:S(2)}) collective-permute-start(bf16[64,1536]{1,0:T(8,128)(2,1)S(1)} %get-tuple-element.648), channel_id=1, source_target_pairs={{7,0},{0,1},{1,2},{2,3},{3,4},{4,5},{5,6},{6,7},{15,8},{8,9},{9,10... | collective-permute-start | bytes 589832 | tf_op jit(solution)/shard_map/while/body/eval_jaxpr/ppermute | solution.py:28
  372.5 8.2 %collective-permute-start = (bf16[64,1536]{1,0:T(8,128)(2,1)S(1)}, bf16[64,1536]{1,0:T(8,128)(2,1)S(1)}, u32[]{:S(2)}, u32[]{:S(2)}) collective-permute-start(bf16[64,1536]{1,0:T(8,128)(2,1)S(1)} %get-tuple-element.648), channel_id=1, source_target_pairs={{7,0},{0,1},{1,2},{2,3},{3,4},{4,5},{5,6},{6,7},{15,8},{8,9},{9,10... | collective-permute-start | bytes 589832 | tf_op jit(solution)/shard_map/while/body/eval_jaxpr/ppermute | solution.py:28
  383.1 13.4 %collective-permute-start = (bf16[64,1536]{1,0:T(8,128)(2,1)S(1)}, bf16[64,1536]{1,0:T(8,128)(2,1)S(1)}, u32[]{:S(2)}, u32[]{:S(2)}) collective-permute-start(bf16[64,1536]{1,0:T(8,128)(2,1)S(1)} %get-tuple-element.648), channel_id=1, source_target_pairs={{7,0},{0,1},{1,2},{2,3},{3,4},{4,5},{5,6},{6,7},{15,8},{8,9},{9,10... | collective-permute-start | bytes 589832 | tf_op jit(solution)/shard_map/while/body/eval_jaxpr/ppermute | solution.py:28
  398.9 12.9 %collective-permute-start = (bf16[64,1536]{1,0:T(8,128)(2,1)S(1)}, bf16[64,1536]{1,0:T(8,128)(2,1)S(1)}, u32[]{:S(2)}, u32[]{:S(2)}) collective-permute-start(bf16[64,1536]{1,0:T(8,128)(2,1)S(1)} %get-tuple-element.648), channel_id=1, source_target_pairs={{7,0},{0,1},{1,2},{2,3},{3,4},{4,5},{5,6},{6,7},{15,8},{8,9},{9,10... | collective-permute-start | bytes 589832 | tf_op jit(solution)/shard_map/while/body/eval_jaxpr/ppermute | solution.py:28
  414.2 16.4 %collective-permute-start = (bf16[64,1536]{1,0:T(8,128)(2,1)S(1)}, bf16[64,1536]{1,0:T(8,128)(2,1)S(1)}, u32[]{:S(2)}, u32[]{:S(2)}) collective-permute-start(bf16[64,1536]{1,0:T(8,128)(2,1)S(1)} %get-tuple-element.648), channel_id=1, source_target_pairs={{7,0},{0,1},{1,2},{2,3},{3,4},{4,5},{5,6},{6,7},{15,8},{8,9},{9,10... | collective-permute-start | bytes 589832 | tf_op jit(solution)/shard_map/while/body/eval_jaxpr/ppermute | solution.py:28
  431.4 1.3 copy-start.8
  433.7 45.3 %all-to-all-start.2 = ((bf16[32,48,192]{2,1,0:T(8,128)(2,1)}), bf16[32,48,192]{2,1,0:T(8,128)(2,1)S(1)}, u32[]{:S(2)}, u32[]{:S(2)}) async-start(bf16[32,48,192]{2,1,0:T(8,128)(2,1)} %broadcast_in_dim.73), calls=%async_computation.2 | async-start | bytes 1572864 | tf_op jit(solution)/shard_map/all_to_all | solution.py:43
  457.7 1.3 copy-start.10
  463.6 15.8 %copy-start.4 = (bf16[192,512]{1,0:T(8,128)(2,1)S(1)}, bf16[192,512]{1,0:T(8,128)(2,1)}, u32[]{:S(2)}) copy-start(bf16[192,512]{1,0:T(8,128)(2,1)} %param.27) | copy-start | bytes 589828
  479.8 67.9 %copy-start.5 = (bf16[192,512]{1,0:T(8,128)(2,1)S(1)}, bf16[192,512]{1,0:T(8,128)(2,1)}, u32[]{:S(2)}) copy-start(bf16[192,512]{1,0:T(8,128)(2,1)} %param.27) | copy-start | bytes 589828
  547.5 15.3 %copy-start.3 = (bf16[4,64,1536]{2,1,0:T(8,128)(2,1)}, bf16[4,64,1536]{2,1,0:T(8,128)(2,1)S(1)}, u32[]{:S(2)}) copy-start(bf16[4,64,1536]{2,1,0:T(8,128)(2,1)S(1)} %slice.46) | copy-start | bytes 2359300
  547.5 4.7 copy-start.13
  547.9 15.1 %copy-start.11 = (f32[512]{0:T(512)S(1)}, f32[512]{0:T(512)}, u32[]{:S(2)}) copy-start(f32[512]{0:T(512)} %param.28) | copy-start | bytes 6148
  548.8 14.0 %all-to-all-start.3 = ((bf16[8,32,1024]{2,1,0:T(8,128)(2,1)}), bf16[8,32,1024]{2,1,0:T(8,128)(2,1)S(1)}, u32[]{:S(2)}, u32[]{:S(2)}) async-start(bf16[8,32,1024]{2,1,0:T(8,128)(2,1)} %bitcast.18), calls=%async_computation.3 | async-start | bytes 1048576 | tf_op jit(solution)/shard_map/all_to_all | solution.py:52
Sparse Core Ops, SparseCore 0:
  432.9 113.4 all-gather.2
